TPU v7x, 512 devices: a whole 4x8x8 slice. The times are simulated.
512 devices in a mesh: row: 16 (over y, z_lo), col: 32 (over x, z_hi, core).
Axes of the slice: x: 4, y: 8, z: 8 (z_hi: 4, z_lo: 2; z = z_hi * 2 + z_lo), core: 2. Of those that a mesh axis runs over, the one named last changes fastest.
Arguments:
- tokens: bfloat16 [512, 12288], P('row', 'col'), may hold values from -6 to 6
- grad_out: bfloat16 [512, 12288], P('row', 'col'), may hold values from -1.796875 to 1.796875
- pre_act: bfloat16 [512, 24576], P('col', 'row'), may hold values from -6 to 6
- w_in: bfloat16 [24576, 12288], P('row', 'col'), may hold values from -0.0546875 to 0.0546875
- w_out: bfloat16 [24576, 12288], P('row', 'col'), may hold values from -0.0390625 to 0.0390625
Outputs:
- grad_tokens: bfloat16 [512, 12288], P('row', 'col')
- grad_w_in: bfloat16 [24576, 12288], P('row', 'col')
- grad_w_out: bfloat16 [24576, 12288], P('row', 'col')
All inputs are finite; a program needn't handle non-finite values.
Results may differ from a plain program's by a relative error of at most 0.005.
Values may be sent and summed in bfloat16 or wider, within the bound.
A program may use at most 64 MiB of HBM per device.

v0:
```python
import jax
import jax.numpy as jnp
from jax import lax
from jax.sharding import PartitionSpec as P

tanh_scale = 0.7978845608028654
cubic_term = 0.044715


def gelu_parts(pre_act):
    pre_value = pre_act.astype(jnp.float32)
    tanh_arg = tanh_scale * (pre_value + cubic_term * pre_value * pre_value * pre_value)
    tangent = jnp.tanh(tanh_arg)
    hidden_value = 0.5 * pre_value * (1.0 + tangent)
    gelu_slope = 0.5 * (1.0 + tangent) + 0.5 * pre_value * (
        1.0 - tangent * tangent
    ) * tanh_scale * (1.0 + 3.0 * cubic_term * pre_value * pre_value)
    return (hidden_value, gelu_slope)


def per_device(tokens, grad_out, pre_act, w_in, w_out):
    contract_rows = (((0,), (0,)), ((), ()))
    contract_cols = (((1,), (1,)), ((), ()))
    out_cols = lax.all_gather(grad_out, "row", axis=0, tiled=True)
    row_block = out_cols
    grad_hidden = lax.psum_scatter(
        lax.dot_general(row_block, w_out, contract_cols, preferred_element_type=jnp.float32),
        "col",
        scatter_dimension=0,
        tiled=True,
    )
    hidden_value, gelu_slope = gelu_parts(pre_act)
    hidden_local = hidden_value.astype(jnp.bfloat16)
    grad_pre_local = (grad_hidden * gelu_slope).astype(jnp.bfloat16)
    hidden_all, grad_pre_all = (
        lax.all_gather(hidden_local, "col", axis=0, tiled=True),
        lax.all_gather(grad_pre_local, "col", axis=0, tiled=True),
    )
    grad_w_out = lax.dot_general(
        hidden_all, out_cols, contract_rows, preferred_element_type=jnp.float32
    ).astype(jnp.bfloat16)
    tok_cols = lax.all_gather(tokens, "row", axis=0, tiled=True)
    grad_w_in = lax.dot_general(
        grad_pre_all, tok_cols, contract_rows, preferred_element_type=jnp.float32
    ).astype(jnp.bfloat16)
    row_block = grad_pre_all
    grad_tokens = lax.psum_scatter(
        jnp.dot(row_block, w_in, preferred_element_type=jnp.float32),
        "row",
        scatter_dimension=0,
        tiled=True,
    ).astype(jnp.bfloat16)
    return (grad_tokens, grad_w_in, grad_w_out)


def solution(mesh):
    in_specs = (P("row", "col"), P("row", "col"), P("col", "row"), P("row", "col"), P("row", "col"))
    out_specs = (P("row", "col"), P("row", "col"), P("row", "col"))
    return jax.shard_map(
        per_device, mesh=mesh, in_specs=in_specs, out_specs=out_specs, check_vma=False
    )
```

profile of v0, /device:TPU:4, one launch (start us, length us, event | category | flops | bytes accessed | tf_op | source)
XLA Modules:
  0.0 355.7 jit_solution(5270605679973017259)
XLA Ops:
  7.2 0.0 copy-start
  7.2 0.0 reduce-scatter.3.cloned.1.call-start
  7.2 37.5 %all_gather.12 = bf16[512,384]{1,0:T(8,128)(2,1)S(1)} all-gather(bf16[32,384]{1,0:T(8,128)(2,1)} %param.6), channel_id=1, replica_groups=mesh['row'=16,'col'=32] {'row'}, dimensions={0}, use_global_device_ids=true | all-gather | bytes 417792 | tf_op jit(solution)/shard_map/all_gather | solution.py:24
  44.7 0.0 copy-done
  44.7 2.6 fusion.11
  47.4 0.0 reduce-scatter.3.cloned.1.call-update
  47.4 0.0 all-gather.3.cloned.1.call-start
  47.4 104.2 %reduce-scatter.3.cloned.1.call-done = f32[16,1536]{1,0:T(8,128)} async-done(((f32[512,1536]{1,0:T(8,128)}), f32[16,1536]{1,0:T(8,128)}) %reduce-scatter.3.cloned.1.call-update) | async-done | bytes 98320 | tf_op jit(solution)/shard_map/reduce_scatter | solution.py:26
  151.6 0.0 copy-done.1
  151.6 1.6 fusion.7
  153.2 0.0 all-gather.3.cloned.1.call-update
  153.3 0.0 all-gather.5.cloned.1.call-start
  153.3 0.7 all-gather.5.cloned.1.call-update
  154.0 0.0 copy-start.2
  154.0 0.0 reduce-scatter.5.cloned.1.call-start
  154.0 57.7 %all-gather.3.cloned.1.call-done = bf16[512,1536]{1,0:T(8,128)(2,1)} async-done(((bf16[16,1536]{1,0:T(8,128)(2,1)}), bf16[512,1536]{1,0:T(8,128)(2,1)}) %all-gather.3.cloned.1.call-update) | async-done | bytes 1572880 | tf_op jit(solution)/shard_map/all_gather | solution.py:37
  211.8 3.7 %fusion.12 = f32[512,384]{1,0:T(8,128)} fusion(bf16[512,1536]{1,0:T(8,128)(2,1)} %all-gather.3.cloned.1.call-done, bf16[1536,384]{1,0:T(8,128)(2,1)} %param.8), kind=kOutput, calls=%fused_computation.21 | convolution fusion | flops 603979776 | bytes 3538944 | tf_op jit(solution)/shard_map/dot_general | solution.py:48
  215.5 0.0 reduce-scatter.5.cloned.1.call-update
  215.5 34.7 %all_gather.14 = bf16[512,384]{1,0:T(8,128)(2,1)S(1)} all-gather(bf16[32,384]{1,0:T(8,128)(2,1)S(1)} %copy-done.2), channel_id=1, replica_groups=mesh['row'=16,'col'=32] {'row'}, dimensions={0}, use_global_device_ids=true | all-gather | bytes 417792 | tf_op jit(solution)/shard_map/all_gather | solution.py:42
  250.2 2.0 convolution_convert_fusion.1
  252.2 20.4 %all-gather.5.cloned.1.call-done = bf16[512,1536]{1,0:T(8,128)(2,1)} async-done(((bf16[16,1536]{1,0:T(8,128)(2,1)}), bf16[512,1536]{1,0:T(8,128)(2,1)}) %all-gather.5.cloned.1.call-update) | async-done | bytes 1572880 | tf_op jit(solution)/shard_map/all_gather | solution.py:36
  272.7 3.4 convolution_convert_fusion
  276.1 71.7 %reduce-scatter.5.cloned.1.call-done = f32[32,384]{1,0:T(8,128)} async-done(((f32[512,384]{1,0:T(8,128)}), f32[32,384]{1,0:T(8,128)}) %reduce-scatter.5.cloned.1.call-update) | async-done | bytes 49168 | tf_op jit(solution)/shard_map/reduce_scatter | solution.py:47
  347.7 1.4 convert_element_type.20
  (4 shorter events, 0.0 us)
Async XLA Ops:
  7.2 37.6 %copy-start = (bf16[1536,384]{1,0:T(8,128)(2,1)S(1)}, bf16[1536,384]{1,0:T(8,128)(2,1)}, u32[]{:S(2)}) copy-start(bf16[1536,384]{1,0:T(8,128)(2,1)} %param.9) | copy-start | bytes 3538948
  7.2 144.4 %reduce-scatter.3.cloned.1.call-start = ((), (), s32[]{:S(2)}) async-start(), calls=%async_computation.2 | async-start | bytes 3244032 | tf_op jit(solution)/shard_map/reduce_scatter | solution.py:26
  47.4 104.3 %copy-start.1 = (bf16[16,1536]{1,0:T(8,128)(2,1)S(1)}, bf16[16,1536]{1,0:T(8,128)(2,1)}, u32[]{:S(2)}) copy-start(bf16[16,1536]{1,0:T(8,128)(2,1)} %param.7) | copy-start | bytes 147460
  47.4 164.4 %all-gather.3.cloned.1.call-start = ((), (), s32[]{:S(2)}) async-start(), calls=%async_computation.3 | async-start | bytes 1622016 | tf_op jit(solution)/shard_map/all_gather | solution.py:37
  153.3 119.4 %all-gather.5.cloned.1.call-start = ((), (), s32[]{:S(2)}) async-start(), calls=%async_computation.5 | async-start | bytes 1622016 | tf_op jit(solution)/shard_map/all_gather | solution.py:36
  154.0 61.5 %copy-start.2 = (bf16[32,384]{1,0:T(8,128)(2,1)S(1)}, bf16[32,384]{1,0:T(8,128)(2,1)}, u32[]{:S(2)}) copy-start(bf16[32,384]{1,0:T(8,128)(2,1)} %param.5) | copy-start | bytes 73732
  154.0 193.7 %reduce-scatter.5.cloned.1.call-start = ((), (), s32[]{:S(2)}) async-start(), calls=%async_computation.4 | async-start | bytes 835584 | tf_op jit(solution)/shard_map/reduce_scatter | solution.py:47
  211.8 38.4 %copy-start.3 = (bf16[512,1536]{1,0:T(8,128)(2,1)S(1)}, bf16[512,1536]{1,0:T(8,128)(2,1)}, u32[]{:S(2)}) copy-start(bf16[512,1536]{1,0:T(8,128)(2,1)} %all-gather.3.cloned.1.call-done) | copy-start | bytes 4718596
Sparse Core Ops, SparseCore 0:
  47.5 104.0 reduce-scatter.2
  155.8 55.9 all-gather.2
  215.9 56.6 all-gather.4
  275.5 72.1 reduce-scatter.4
where the time goes:
time: 356 us
  waiting for transfers between devices  255 us (72%)
  blocking collectives  72.2 us (20%)
  between operations  13.8 us (4%)
  matrix products  11.8 us (3%)
    reduce_scatter x1, waiting for transfers between devices, per_device(): lax.psum_scatter(lax.dot_general(row_block, w_out, contract_cols, preferr...  104 us
    reduce_scatter x1, waiting for transfers between devices, per_device(): lax.psum_scatter(jnp.dot(row_block, w_in, preferred_element_type=jnp.floa...  71.7 us
    all_gather x1, waiting for transfers between devices, per_device(): lax.all_gather(grad_pre_local, 'col', axis=0, tiled=True)  57.7 us
    all_gather x1, blocking collectives, per_device(): out_cols = lax.all_gather(grad_out, 'row', axis=0, tiled=True)  37.5 us
    all_gather x1, blocking collectives, per_device(): tok_cols = lax.all_gather(tokens, 'row', axis=0, tiled=True)  34.7 us
    all_gather x1, waiting for transfers between devices, per_device(): lax.all_gather(hidden_local, 'col', axis=0, tiled=True)  20.4 us
  transfers between devices with their start and end apart: 4, of which 4 were waited for; matrix products, arithmetic and copies ran while one was open for 3% of the time, Pallas kernels for 0%

commit v1 on v0

v1 whole, which is shorter than its diff:
```python
import jax
import jax.numpy as jnp
from jax import lax
from jax.experimental import pallas as pl
from jax.experimental.pallas import tpu as pltpu
from jax.sharding import PartitionSpec as P

tanh_scale = 0.7978845608028654
cubic_term = 0.044715

MESH = pl.DeviceIdType.MESH
F32 = jnp.float32
BF16 = jnp.bfloat16
NX, NZ, NY = 4, 4, 8
FEAT = 384
HID = 1536
HQ = HID // NX
FAR_FIRST = (4, 3, 5, 2, 6, 1, 7)
NEAR_FIRST = (1, 7, 2, 6, 3, 5, 4)
X_ORDER = (2, 1, 3)
Z_ORDER = (2, 1, 3)


def gelu_hidden(u):
    q = jnp.tanh(tanh_scale * (u + cubic_term * u * u * u))
    return 0.5 * u * (1.0 + q)


def gelu_slope(u):
    q = jnp.tanh(tanh_scale * (u + cubic_term * u * u * u))
    return 0.5 * (1.0 + q) + 0.5 * u * (1.0 - q * q) * tanh_scale * (1.0 + 3.0 * cubic_term * u * u)


def kernel(
    tok_hbm, go_hbm, pre_hbm, win_hbm, wout_hbm,
    gt_hbm, gwi_hbm, gwo_hbm,
    tok_own, go_own, pre_own, wo2, wi2, go, go_sib, tok, pre, part, part_f, rx, sb, rz,
    gp, gp_sib, hid, hid_sib, fb, gz, gb, gy, gt_out, gwi_out, gwo_out,
    local, a_s, a_r, az_s, az_r, x_s, x_r, z_s, z_r, p_s, p_r, hz_s, hz_r, hx_s, hx_r,
    ez_s, ez_r, ex_s, ex_r, gz_s, gz_r, gy_s, gy_r, t_s, t_r, tz_s, tz_r, c_s, c_r,
):
    r, c = lax.axis_index("row"), lax.axis_index("col")
    y, zl = r // 2, r % 2
    x, zh, k = c // 8, (c // 2) % NZ, c % 2

    def dev(dy=0, dzl=0, dx=0, dz=0, core=None):
        yy, ll = (y + dy) % NY, (zl + dzl) % 2
        xx, hh = (x + dx) % NX, (zh + dz) % NZ
        kk = k if core is None else core
        return (yy * 2 + ll, (xx * NZ + hh) * 2 + kk)

    def slot(yy, ll):
        return ((yy % 2) * 2 + ll) * NX + yy // 2

    def rows(start, size):
        return pl.ds(pl.multiple_of(start, 16), size)

    def cols(index, size):
        return pl.ds(pl.multiple_of(index * size, 128), size)

    sends = []

    def send(src, dst, ssem, rsem, to):
        cp = pltpu.make_async_remote_copy(
            src_ref=src, dst_ref=dst, send_sem=ssem, recv_sem=rsem, device_id=to, device_id_type=MESH
        )
        cp.start()
        sends.append((src, ssem))

    def arrived(ref, sem):
        pltpu.make_async_copy(ref, ref, sem).wait()

    sib = dev(core=1 - k)
    mine = slot(y, zl)

    peers = [dev(dy=d, core=kk) for d in range(1, NY) for kk in range(2)]
    peers += [dev(dzl=1, core=kk) for kk in range(2)] + [sib]
    peers += [dev(dx=d) for d in range(1, NX)] + [dev(dz=d) for d in range(1, NZ)]
    barrier = pltpu.get_barrier_semaphore()
    for to in peers:
        pl.semaphore_signal(barrier, inc=1, device_id=to, device_id_type=MESH)

    loads = [
        pltpu.make_async_copy(pre_hbm, pre_own, local.at[0]),
        pltpu.make_async_copy(go_hbm, go_own, local.at[1]),
        pltpu.make_async_copy(tok_hbm, tok_own, local.at[2]),
        pltpu.make_async_copy(wout_hbm, wo2.at[:, cols(k, FEAT)], local.at[3]),
        pltpu.make_async_copy(win_hbm, wi2.at[:, cols(k, FEAT)], local.at[4]),
    ]
    for cp in loads:
        cp.start()
    loads[0].wait()
    loads[1].wait()
    my_rows = rows(16 * (zh * NX + x), 16)
    hid[my_rows, :] = gelu_hidden(pre_own[...].astype(F32)).astype(BF16)
    pre[rows(16 * x, 16), :] = pre_own[:, cols(x, HQ)]
    go[rows(16 * mine, 16), cols(k, FEAT)] = go_own[k]
    pl.semaphore_wait(barrier, len(peers))

    send(go_own.at[1 - k], go.at[rows(16 * mine, 16), cols(k, FEAT)], c_s.at[0], c_r.at[0], sib)
    for d in FAR_FIRST:
        for kk in range(2):
            send(go_own.at[kk], go.at[rows(16 * mine, 16), cols(k, FEAT)], a_s.at[d, kk], a_r.at[d], dev(dy=d, core=kk))
    for kk in range(2):
        send(go_own.at[kk], go.at[rows(16 * mine, 16), cols(k, FEAT)], az_s.at[0, kk], az_r.at[0], dev(dzl=1, core=kk))
    send(wout_hbm, wo2.at[:, cols(k, FEAT)], c_s.at[1], c_r.at[1], sib)
    for d in X_ORDER:
        send(pre_own.at[:, cols((x + d) % NX, HQ)], pre.at[rows(16 * x, 16), :], p_s.at[d], p_r.at[d], dev(dx=d))
    for d in Z_ORDER:
        send(hid.at[my_rows], hid.at[my_rows], hz_s.at[d], hz_r.at[d], dev(dz=d))
    for d in X_ORDER:
        send(hid.at[my_rows], hid.at[my_rows], hx_s.at[0, d], hx_r.at[0, d], dev(dx=d))
    for d in NEAR_FIRST:
        block = go.at[rows(16 * slot((y - d) % NY, zl), 16), :]
        arrived(block, a_r.at[d])
        send(block, block, az_s.at[d, 0], az_r.at[d], dev(dzl=1))
    arrived(go.at[rows(16 * mine, 16), cols(1 - k, FEAT)], c_r.at[0])
    loads[3].wait()
    arrived(wo2.at[:, cols(1 - k, FEAT)], c_r.at[1])
    for d in (0,) + NEAR_FIRST:
        arrived(go.at[rows(16 * slot((y - d) % NY, 1 - zl), 16), :], az_r.at[d])

    for dz in Z_ORDER + (0,):
        t = rows(64 * ((zh + dz) % NZ), 64)
        for dx in X_ORDER + (0,):
            xx = (x + dx) % NX
            product = lax.dot_general(
                go[t, :], wo2[rows(HQ * xx, HQ), :], (((1,), (1,)), ((), ())), preferred_element_type=F32
            )
            if dx:
                part[xx, t, :] = product.astype(BF16)
                send(part.at[xx, t], rx.at[dx - 1, t], x_s.at[dz, dx], x_r.at[dz, dx], dev(dx=dx))
            else:
                part_f[t, :] = product

    send(go.at[:, cols(1 - k, FEAT)], go_sib, c_s.at[2], c_r.at[2], sib)
    send(win_hbm, wi2.at[:, cols(k, FEAT)], c_s.at[3], c_r.at[3], sib)
    loads[2].wait()
    tok[mine] = tok_own[...]
    for d in FAR_FIRST:
        send(tok_own, tok.at[mine], t_s.at[d], t_r.at[d], dev(dy=d))
    send(tok_own, tok.at[mine], tz_s.at[0], tz_r.at[0], dev(dzl=1))

    for dz in Z_ORDER + (0,):
        t = rows(64 * ((zh + dz) % NZ), 64)
        for dx in X_ORDER:
            arrived(rx.at[dx - 1, t], x_r.at[dz, dx])
        total = part_f[t, :] + rx[0, t, :].astype(F32) + rx[1, t, :].astype(F32) + rx[2, t, :].astype(F32)
        if dz:
            sb[dz - 1] = total.astype(BF16)
            send(sb.at[dz - 1], rz.at[dz - 1], z_s.at[dz], z_r.at[dz], dev(dz=dz))
        else:
            part_f[t, :] = total

    for dz in (1, 3, 2):
        block = hid.at[rows(16 * (((zh - dz) % NZ) * NX + x), 16)]
        arrived(block, hz_r.at[dz])
        for dx in X_ORDER:
            send(block, block, hx_s.at[dz, dx], hx_r.at[dz, dx], dev(dx=dx))

    for d in X_ORDER:
        arrived(pre.at[rows(16 * ((x - d) % NX), 16), :], p_r.at[d])
    slope = gelu_slope(pre[...].astype(F32))
    for d in (1, 3, 2):
        arrived(rz.at[d - 1], z_r.at[d])
    t = rows(64 * zh, 64)
    total = part_f[t, :] + rz[0].astype(F32) + rz[1].astype(F32) + rz[2].astype(F32)
    gp[t, cols(x, HQ)] = (total * slope).astype(BF16)

    block = gp.at[t, cols(x, HQ)]
    for d in Z_ORDER:
        send(block, block, ez_s.at[d], ez_r.at[d], dev(dz=d))
    for d in X_ORDER:
        send(block, block, ex_s.at[0, d], ex_r.at[0, d], dev(dx=d))
    for d in NEAR_FIRST:
        block = tok.at[slot((y - d) % NY, zl)]
        arrived(block, t_r.at[d])
        send(block, block, tz_s.at[d], tz_r.at[d], dev(dzl=1))
    for dz in (1, 3, 2):
        block = gp.at[rows(64 * ((zh - dz) % NZ), 64), cols(x, HQ)]
        arrived(block, ez_r.at[dz])
        for dx in X_ORDER:
            send(block, block, ex_s.at[dz, dx], ex_r.at[dz, dx], dev(dx=dx))

    for dz in range(NZ):
        for dx in X_ORDER:
            arrived(hid.at[rows(16 * (((zh - dz) % NZ) * NX + (x - dx) % NX), 16)], hx_r.at[dz, dx])
    send(hid, hid_sib, c_s.at[4], c_r.at[4], sib)

    loads[4].wait()
    arrived(wi2.at[:, cols(1 - k, FEAT)], c_r.at[3])

    def grad_tokens_part(wave):
        t = rows(64 * wave, 64)
        dz = (zh - wave) % NZ
        for dx in X_ORDER:
            arrived(gp.at[t, cols((x - dx) % NX, HQ)], ex_r.at[dz, dx])
        return jnp.dot(gp[t, :], wi2[...], preferred_element_type=F32)

    for odd in (1, 0):
        fb[odd] = grad_tokens_part((1 - zl) + 2 * ((y + odd) % 2)).astype(BF16)
        send(fb.at[odd], gz.at[odd], gz_s.at[odd], gz_r.at[odd], dev(dzl=1))
    for odd in (1, 0):
        mine_part = grad_tokens_part(zl + 2 * ((y + odd) % 2))
        arrived(gz.at[odd], gz_r.at[odd])
        gb[odd] = (mine_part + gz[odd].astype(F32)).astype(BF16)
        for d in ((3, 5, 1, 7) if odd else (4, 2, 6)):
            t = rows(16 * (((y + d) % NY) // 2), 16)
            for kk in range(2):
                send(
                    gb.at[odd, t, pl.ds(FEAT * kk, FEAT)], gy.at[d, k], gy_s.at[d, kk], gy_r.at[d], dev(dy=d, core=kk)
                )
        if not odd:
            t = rows(16 * (y // 2), 16)
            gy[0, k] = gb[0, t, cols(k, FEAT)]
            send(gb.at[0, t, cols(1 - k, FEAT)], gy.at[0, k], gy_s.at[0, 0], gy_r.at[0], sib)
    send(gp, gp_sib, c_s.at[5], c_r.at[5], sib)

    over_tokens = (((0,), (0,)), ((), ()))
    arrived(go_sib, c_r.at[2])
    arrived(hid_sib, c_r.at[4])
    for h in range(0, HID, 256):
        a = lax.dot_general(hid[:, h : h + 256], go[:, cols(k, FEAT)], over_tokens, preferred_element_type=F32)
        b = lax.dot_general(hid_sib[:, h : h + 256], go_sib[...], over_tokens, preferred_element_type=F32)
        gwo_out[h : h + 256, :] = (a + b).astype(BF16)
    store_gwo = pltpu.make_async_copy(gwo_out, gwo_hbm, local.at[5])
    store_gwo.start()
    for d in (0,) + NEAR_FIRST:
        arrived(tok.at[slot((y - d) % NY, 1 - zl)], tz_r.at[d])
    arrived(gp_sib, c_r.at[5])
    tok_mine = tok[:, k].reshape(256, FEAT)
    tok_other = tok[:, 1 - k].reshape(256, FEAT)
    for h in range(0, HID, 256):
        a = lax.dot_general(gp[:, h : h + 256], tok_mine, over_tokens, preferred_element_type=F32)
        b = lax.dot_general(gp_sib[:, h : h + 256], tok_other, over_tokens, preferred_element_type=F32)
        gwi_out[h : h + 256, :] = (a + b).astype(BF16)
    store_gwi = pltpu.make_async_copy(gwi_out, gwi_hbm, local.at[6])
    store_gwi.start()

    arrived(gy.at[0, 1 - k], gy_r.at[0])
    total = gy[0].astype(F32)
    for d in NEAR_FIRST:
        arrived(gy.at[d], gy_r.at[d])
        total += gy[d].astype(F32)
    gt_out[...] = total.astype(BF16)
    store_gt = pltpu.make_async_copy(gt_out, gt_hbm, local.at[7])
    store_gt.start()
    for src, ssem in sends:
        arrived(src, ssem)
    store_gwo.wait()
    store_gwi.wait()
    store_gt.wait()


def per_device(tokens, grad_out, pre_act, w_in, w_out):
    vmem = pltpu.VMEM
    dma = pltpu.SemaphoreType.DMA
    any_space = pl.BlockSpec(memory_space=pl.ANY)
    scratch = [
        vmem((2, 16, FEAT), BF16),
        vmem((2, 16, FEAT), BF16),
        vmem((16, HID), BF16),
        vmem((HID, 2 * FEAT), BF16),
        vmem((HID, 2 * FEAT), BF16),
        vmem((256, 2 * FEAT), BF16),
        vmem((256, FEAT), BF16),
        vmem((16, 2, 16, FEAT), BF16),
        vmem((64, HQ), BF16),
        vmem((NX, 256, HQ), BF16),
        vmem((256, HQ), F32),
        vmem((NX - 1, 256, HQ), BF16),
        vmem((NZ - 1, 64, HQ), BF16),
        vmem((NZ - 1, 64, HQ), BF16),
        vmem((256, HID), BF16),
        vmem((256, HID), BF16),
        vmem((256, HID), BF16),
        vmem((256, HID), BF16),
        vmem((2, 64, 2 * FEAT), BF16),
        vmem((2, 64, 2 * FEAT), BF16),
        vmem((2, 64, 2 * FEAT), BF16),
        vmem((NY, 2, 16, FEAT), BF16),
        vmem((2, 16, FEAT), BF16),
        vmem((HID, FEAT), BF16),
        vmem((HID, FEAT), BF16),
        dma((8,)),
        dma((NY, 2)), dma((NY,)),
        dma((NY, 2)), dma((NY,)),
        dma((NZ, NX)), dma((NZ, NX)),
        dma((NZ,)), dma((NZ,)),
        dma((NX,)), dma((NX,)),
        dma((NZ,)), dma((NZ,)),
        dma((NZ, NX)), dma((NZ, NX)),
        dma((NZ,)), dma((NZ,)),
        dma((NZ, NX)), dma((NZ, NX)),
        dma((2,)), dma((2,)),
        dma((NY, 2)), dma((NY,)),
        dma((NY,)), dma((NY,)),
        dma((NY,)), dma((NY,)),
        dma((6,)), dma((6,)),
    ]
    grad_tokens, grad_w_in, grad_w_out = pl.pallas_call(
        kernel,
        out_shape=(
            jax.ShapeDtypeStruct((2, 16, FEAT), BF16),
            jax.ShapeDtypeStruct((HID, FEAT), BF16),
            jax.ShapeDtypeStruct((HID, FEAT), BF16),
        ),
        in_specs=[any_space] * 5,
        out_specs=(any_space,) * 3,
        scratch_shapes=scratch,
        compiler_params=pltpu.CompilerParams(
            collective_id=0, has_side_effects=True, vmem_limit_bytes=40 * 2**20
        ),
    )(tokens.reshape(2, 16, FEAT), grad_out.reshape(2, 16, FEAT), pre_act, w_in, w_out)
    return grad_tokens.reshape(32, FEAT), grad_w_in, grad_w_out


def solution(mesh):
    in_specs = (P("row", "col"), P("row", "col"), P("col", "row"), P("row", "col"), P("row", "col"))
    out_specs = (P("row", "col"), P("row", "col"), P("row", "col"))
    return jax.shard_map(per_device, mesh=mesh, in_specs=in_specs, out_specs=out_specs, check_vma=False)
```

time: 356 us -> 75.3 us (0.21)
  the two profiles are of different devices: /device:TPU:4 before, /device:TPU:1 now
where the time goes in v1:
time: 75.3 us; the launch traced here: 74.9 us
  Pallas kernels  66.8 us (89%)
  local copies, waits for them, and re-layouts  7.44 us (10%)
    pallas_call x1, Pallas kernels, per_device(): pl.pallas_call(kernel, out_shape=(jax.ShapeDtypeStruct((2, 16, FEAT), BF1...  66.8 us
    unnamed x13, local copies, waits for them, and re-layouts  7.44 us

profile of v1, /device:TPU:1, one launch (start us, length us, event | category | flops | bytes accessed | tf_op | source)
XLA Modules:
  0.0 74.9 jit_solution(5988500102007619950)
XLA Ops:
  0.6 0.0 copy-start
  0.6 1.3 %copy-done = bf16[1536,384]{1,0:T(8,128)(2,1)S(1)} copy-done((bf16[1536,384]{1,0:T(8,128)(2,1)S(1)}, bf16[1536,384]{1,0:T(8,128)(2,1)}, u32[]{:S(2)}) %copy-start) | copy-done | bytes 1179672
  1.9 0.0 copy-start.1
  1.9 1.3 %copy-done.1 = bf16[1536,384]{1,0:T(8,128)(2,1)S(1)} copy-done((bf16[1536,384]{1,0:T(8,128)(2,1)S(1)}, bf16[1536,384]{1,0:T(8,128)(2,1)}, u32[]{:S(2)}) %copy-start.1) | copy-done | bytes 1179672
  3.2 0.0 copy-start.2
  3.2 0.8 %copy-done.2 = bf16[16,1536]{1,0:T(8,128)(2,1)S(1)} copy-done((bf16[16,1536]{1,0:T(8,128)(2,1)S(1)}, bf16[16,1536]{1,0:T(8,128)(2,1)}, u32[]{:S(2)}) %copy-start.2) | copy-done | bytes 49176
  4.0 0.0 copy-start.3
  4.0 0.7 copy-done.3
  4.7 0.0 copy-start.4
  4.7 0.7 copy-done.4
  5.4 66.8 %shard_map.76 = (bf16[2,16,384]{2,1,0:T(8,128)(2,1)S(1)}, bf16[1536,384]{1,0:T(8,128)(2,1)S(1)}, bf16[1536,384]{1,0:T(8,128)(2,1)S(1)}) custom-call(bf16[2,16,384]{2,1,0:T(8,128)(2,1)S(1)} %bitcast.3, bf16[2,16,384]{2,1,0:T(8,128)(2,1)S(1)} %bitcast.4, bf16[16,1536]{1,0:T(8,128)(2,1)S(1)} %copy-done.2, bf16[1536,384]{1,0:T(8,128)(2,1)S(1)} %copy-done, ...), custom_call_target="tpu_custom_call" | custom-call | tf_op jit(solution)/shard_map/pallas_call | solution.py:301
  72.2 0.6 copy.11
  72.9 1.0 %copy.12 = bf16[1536,384]{1,0:T(8,128)(2,1)} copy(bf16[1536,384]{1,0:T(8,128)(2,1)S(1)} %get-tuple-element.13) | data formatting | bytes 2359296
  73.9 1.0 %copy.13 = bf16[1536,384]{1,0:T(8,128)(2,1)} copy(bf16[1536,384]{1,0:T(8,128)(2,1)S(1)} %get-tuple-element.14) | data formatting | bytes 2359296
Async XLA Ops:
  0.6 1.3 %copy-start = (bf16[1536,384]{1,0:T(8,128)(2,1)S(1)}, bf16[1536,384]{1,0:T(8,128)(2,1)}, u32[]{:S(2)}) copy-start(bf16[1536,384]{1,0:T(8,128)(2,1)} %win_hbm.1) | copy-start | bytes 3538948
  1.9 1.3 %copy-start.1 = (bf16[1536,384]{1,0:T(8,128)(2,1)S(1)}, bf16[1536,384]{1,0:T(8,128)(2,1)}, u32[]{:S(2)}) copy-start(bf16[1536,384]{1,0:T(8,128)(2,1)} %wout_hbm.1) | copy-start | bytes 3538948
  3.2 0.8 %copy-start.2 = (bf16[16,1536]{1,0:T(8,128)(2,1)S(1)}, bf16[16,1536]{1,0:T(8,128)(2,1)}, u32[]{:S(2)}) copy-start(bf16[16,1536]{1,0:T(8,128)(2,1)} %pre_hbm.1) | copy-start | bytes 147460
  4.0 0.7 copy-start.3
  4.7 0.7 copy-start.4

commit v2 on v1

v2 whole, which is shorter than its diff:
```python
import jax
import jax.numpy as jnp
from jax import lax
from jax.experimental import pallas as pl
from jax.experimental.pallas import tpu as pltpu
from jax.sharding import PartitionSpec as P

tanh_scale = 0.7978845608028654
cubic_term = 0.044715

MESH = pl.DeviceIdType.MESH
F32 = jnp.float32
BF16 = jnp.bfloat16
NX, NZ, NY = 4, 4, 8
FEAT = 384
HID = 1536
HQ = HID // NX
FAR_FIRST = (4, 3, 5, 2, 6, 1, 7)
Y_ODD = (3, 5, 1, 7)
Y_EVEN = (4, 2, 6)
X_ORDER = (2, 1, 3)
Z_ORDER = (2, 1, 3)


def gelu_hidden(u):
    q = jnp.tanh(tanh_scale * (u + cubic_term * u * u * u))
    return 0.5 * u * (1.0 + q)


def gelu_slope(u):
    q = jnp.tanh(tanh_scale * (u + cubic_term * u * u * u))
    return 0.5 * (1.0 + q) + 0.5 * u * (1.0 - q * q) * tanh_scale * (1.0 + 3.0 * cubic_term * u * u)


def kernel(
    tok_hbm, go_hbm, pre_hbm, win_hbm, wout_hbm,
    gt_out, gwi_out, gwo_out,
    tok_own, go_own, pre_own, wo2, wi2, go, go_sib, tok, pre, part, part_f, rx, sb, rz,
    gp, gp_sib, hid, hid_sib, fb, gy,
    local, a_s, a_r, az_s, az_r, x_s, x_r, z_s, z_r, p_s, p_r, hz_s, hz_r, hx_s, hx_r,
    ez_s, ez_r, ex_s, ex_r, gy_s, gy_r, t_s, t_r, tz_s, tz_r, c_s, c_r,
):
    r, c = lax.axis_index("row"), lax.axis_index("col")
    y, zl = r // 2, r % 2
    x, zh, k = c // 8, (c // 2) % NZ, c % 2

    def dev(dy=0, dzl=0, dx=0, dz=0, core=None):
        yy, ll = (y + dy) % NY, (zl + dzl) % 2
        xx, hh = (x + dx) % NX, (zh + dz) % NZ
        kk = k if core is None else core
        return (yy * 2 + ll, (xx * NZ + hh) * 2 + kk)

    def slot(yy, ll):
        return ((yy % 2) * 2 + ll) * NX + yy // 2

    def rows(start, size):
        return pl.ds(pl.multiple_of(start, 16), size)

    def cols(index, size):
        return pl.ds(pl.multiple_of(index * size, 128), size)

    sends = []

    def send(src, dst, ssem, rsem, to):
        cp = pltpu.make_async_remote_copy(
            src_ref=src, dst_ref=dst, send_sem=ssem, recv_sem=rsem, device_id=to, device_id_type=MESH
        )
        cp.start()
        sends.append((src, ssem))

    def arrived(ref, sem):
        pltpu.make_async_copy(ref, ref, sem).wait()

    sib = dev(core=1 - k)
    mine = slot(y, zl)

    peers = [dev(dy=d, core=kk) for d in range(1, NY) for kk in range(2)]
    peers += [dev(dzl=1, core=kk) for kk in range(2)] + [sib]
    peers += [dev(dx=d) for d in range(1, NX)] + [dev(dz=d) for d in range(1, NZ)]
    barrier = pltpu.get_barrier_semaphore()
    for to in peers:
        pl.semaphore_signal(barrier, inc=1, device_id=to, device_id_type=MESH)

    loads = [
        pltpu.make_async_copy(pre_hbm, pre_own, local.at[0]),
        pltpu.make_async_copy(go_hbm, go_own, local.at[1]),
        pltpu.make_async_copy(tok_hbm, tok_own, local.at[2]),
        pltpu.make_async_copy(wout_hbm, wo2.at[:, cols(k, FEAT)], local.at[3]),
        pltpu.make_async_copy(win_hbm, wi2.at[:, cols(k, FEAT)], local.at[4]),
    ]
    for cp in loads:
        cp.start()
    loads[0].wait()
    loads[1].wait()
    my_rows = rows(16 * (zh * NX + x), 16)
    hid[my_rows, :] = gelu_hidden(pre_own[...].astype(F32)).astype(BF16)
    pre[rows(16 * x, 16), :] = pre_own[:, cols(x, HQ)]
    go[rows(16 * mine, 16), cols(k, FEAT)] = go_own[k]
    pl.semaphore_wait(barrier, len(peers))

    send(wout_hbm, wo2.at[:, cols(k, FEAT)], c_s.at[1], c_r.at[1], sib)
    send(go_own.at[1 - k], go.at[rows(16 * mine, 16), cols(k, FEAT)], c_s.at[0], c_r.at[0], sib)
    for d in Y_ODD + Y_EVEN:
        for kk in range(2):
            send(go_own.at[kk], go.at[rows(16 * mine, 16), cols(k, FEAT)], a_s.at[d, kk], a_r.at[d], dev(dy=d, core=kk))
    for kk in range(2):
        send(go_own.at[kk], go.at[rows(16 * mine, 16), cols(k, FEAT)], az_s.at[0, kk], az_r.at[0], dev(dzl=1, core=kk))
    for d in Z_ORDER:
        send(hid.at[my_rows], hid.at[my_rows], hz_s.at[d], hz_r.at[d], dev(dz=d))
    for d in X_ORDER:
        send(pre_own.at[:, cols((x + d) % NX, HQ)], pre.at[rows(16 * x, 16), :], p_s.at[d], p_r.at[d], dev(dx=d))
    for d in X_ORDER:
        send(hid.at[my_rows], hid.at[my_rows], hx_s.at[0, d], hx_r.at[0, d], dev(dx=d))

    def zh_of(wave):
        return ((y + 1 - wave % 2) % 2) * 2 + (zl + wave // 2) % 2

    for wave in range(4):
        for d in Y_ODD if wave % 2 == 0 else Y_EVEN:
            block = go.at[rows(16 * slot((y + NY - d) % NY, (zl + wave // 2) % 2), 16), :]
            if wave < 2:
                arrived(block, a_r.at[d])
                send(block, block, az_s.at[d, 0], az_r.at[d], dev(dzl=1))
            else:
                arrived(block, az_r.at[d])
        if wave == 0:
            loads[3].wait()
            arrived(wo2.at[:, cols(1 - k, FEAT)], c_r.at[1])
        if wave == 1:
            arrived(go.at[rows(16 * mine, 16), cols(1 - k, FEAT)], c_r.at[0])
        if wave == 3:
            arrived(go.at[rows(16 * slot(y, 1 - zl), 16), :], az_r.at[0])
        t = rows(64 * zh_of(wave), 64)
        for dx in X_ORDER + (0,):
            xx = (x + dx) % NX
            product = lax.dot_general(
                go[t, :], wo2[rows(HQ * xx, HQ), :], (((1,), (1,)), ((), ())), preferred_element_type=F32
            )
            if dx:
                part[xx, t, :] = product.astype(BF16)
                send(part.at[xx, t], rx.at[dx - 1, t], x_s.at[wave, dx], x_r.at[wave, dx], dev(dx=dx))
            else:
                part_f[t, :] = product

    send(go.at[:, cols(1 - k, FEAT)], go_sib, c_s.at[2], c_r.at[2], sib)
    send(win_hbm, wi2.at[:, cols(k, FEAT)], c_s.at[3], c_r.at[3], sib)
    loads[2].wait()
    tok[mine] = tok_own[...]
    for d in FAR_FIRST:
        send(tok_own, tok.at[mine], t_s.at[d], t_r.at[d], dev(dy=d))
    send(tok_own, tok.at[mine], tz_s.at[0], tz_r.at[0], dev(dzl=1))

    my_wave = ((zh + zl) % 2) * 2 + (zh // 2 + y + 1) % 2

    def other(index):
        return index + jnp.where(index >= my_wave, 1, 0)

    def summed_over_x(wave):
        t = rows(64 * zh_of(wave), 64)
        for dx in X_ORDER:
            arrived(rx.at[dx - 1, t], x_r.at[wave, dx])
        return part_f[t, :] + rx[0, t, :].astype(F32) + rx[1, t, :].astype(F32) + rx[2, t, :].astype(F32)

    for index in range(3):
        wave = other(index)
        sb[index] = summed_over_x(wave).astype(BF16)
        dz = (zh_of(wave) + NZ - zh) % NZ
        send(sb.at[index], rz.at[dz - 1], z_s.at[dz], z_r.at[dz], dev(dz=dz))
    total = summed_over_x(my_wave)

    for dz in (1, 3, 2):
        block = hid.at[rows(16 * (((zh + NZ - dz) % NZ) * NX + x), 16)]
        arrived(block, hz_r.at[dz])
        for dx in X_ORDER:
            send(block, block, hx_s.at[dz, dx], hx_r.at[dz, dx], dev(dx=dx))

    for d in X_ORDER:
        arrived(pre.at[rows(16 * ((x + NX - d) % NX), 16), :], p_r.at[d])
    slope = gelu_slope(pre[...].astype(F32))
    for d in (1, 3, 2):
        arrived(rz.at[d - 1], z_r.at[d])
    t = rows(64 * zh, 64)
    total += rz[0].astype(F32) + rz[1].astype(F32) + rz[2].astype(F32)
    gp[t, cols(x, HQ)] = (total * slope).astype(BF16)

    block = gp.at[t, cols(x, HQ)]
    for d in Z_ORDER:
        send(block, block, ez_s.at[d], ez_r.at[d], dev(dz=d))
    for d in X_ORDER:
        send(block, block, ex_s.at[0, d], ex_r.at[0, d], dev(dx=d))
    for d in FAR_FIRST:
        block = tok.at[slot((y + NY - d) % NY, zl)]
        arrived(block, t_r.at[d])
        send(block, block, tz_s.at[d], tz_r.at[d], dev(dzl=1))
    for index in range(3):
        origin = zh_of(other(index))
        dz = (zh + NZ - origin) % NZ
        block = gp.at[rows(64 * origin, 64), cols(x, HQ)]
        arrived(block, ez_r.at[dz])
        for dx in X_ORDER:
            send(block, block, ex_s.at[dz, dx], ex_r.at[dz, dx], dev(dx=dx))

    for dz in range(NZ):
        for dx in X_ORDER:
            arrived(hid.at[rows(16 * (((zh + NZ - dz) % NZ) * NX + (x + NX - dx) % NX), 16)], hx_r.at[dz, dx])
    send(hid, hid_sib, c_s.at[4], c_r.at[4], sib)

    loads[4].wait()
    arrived(wi2.at[:, cols(1 - k, FEAT)], c_r.at[3])
    for wave in range(4):
        zw = zh_of(wave)
        t = rows(64 * zw, 64)
        dz = (zh + NZ - zw) % NZ
        for dx in X_ORDER:
            arrived(gp.at[t, cols((x + NX - dx) % NX, HQ)], ex_r.at[dz, dx])
        fb[wave] = jnp.dot(gp[t, :], wi2[...], preferred_element_type=F32).astype(BF16)
        far = wave // 2
        for d in Y_ODD if wave % 2 == 0 else Y_EVEN + (0,):
            at = rows(16 * (((y + d) % NY) // 2), 16)
            for flip in range(2):
                kk = k if flip == 0 else 1 - k
                src = fb.at[wave, at, cols(kk, FEAT)]
                if d or far or flip:
                    send(src, gy.at[far, d, k], gy_s.at[far, d, flip], gy_r.at[far, d], dev(dy=d, dzl=far, core=kk))
                else:
                    gy[0, 0, k] = fb[wave, at, cols(kk, FEAT)]
    send(gp, gp_sib, c_s.at[5], c_r.at[5], sib)

    over_tokens = (((0,), (0,)), ((), ()))
    arrived(go_sib, c_r.at[2])
    arrived(hid_sib, c_r.at[4])
    for h in range(0, HID, 256):
        a = lax.dot_general(hid[:, h : h + 256], go[:, cols(k, FEAT)], over_tokens, preferred_element_type=F32)
        b = lax.dot_general(hid_sib[:, h : h + 256], go_sib[...], over_tokens, preferred_element_type=F32)
        gwo_out[h : h + 256, :] = (a + b).astype(BF16)
    for d in (0,) + FAR_FIRST:
        arrived(tok.at[slot((y + NY - d) % NY, 1 - zl)], tz_r.at[d])
    arrived(gp_sib, c_r.at[5])
    tok_mine = tok[:, k].reshape(256, FEAT)
    tok_other = tok[:, 1 - k].reshape(256, FEAT)
    for h in range(0, HID, 256):
        a = lax.dot_general(gp[:, h : h + 256], tok_mine, over_tokens, preferred_element_type=F32)
        b = lax.dot_general(gp_sib[:, h : h + 256], tok_other, over_tokens, preferred_element_type=F32)
        gwi_out[h : h + 256, :] = (a + b).astype(BF16)

    arrived(gy.at[0, 0, 1 - k], gy_r.at[0, 0])
    total = gy[0, 0].astype(F32)
    for far in range(2):
        for d in Y_ODD + Y_EVEN + ((0,) if far else ()):
            arrived(gy.at[far, d], gy_r.at[far, d])
            total += gy[far, d].astype(F32)
    gt_out[...] = total.astype(BF16)
    for src, ssem in sends:
        arrived(src, ssem)


def store_kernel(*refs):
    sem = refs[-1]
    copies = [pltpu.make_async_copy(refs[i], refs[3 + i], sem.at[i]) for i in range(3)]
    for cp in copies:
        cp.start()
    for cp in copies:
        cp.wait()


def per_device(tokens, grad_out, pre_act, w_in, w_out):
    vmem = pltpu.VMEM
    dma = pltpu.SemaphoreType.DMA
    any_space = pl.BlockSpec(memory_space=pl.ANY)
    scratch = [
        vmem((2, 16, FEAT), BF16),
        vmem((2, 16, FEAT), BF16),
        vmem((16, HID), BF16),
        vmem((HID, 2 * FEAT), BF16),
        vmem((HID, 2 * FEAT), BF16),
        vmem((256, 2 * FEAT), BF16),
        vmem((256, FEAT), BF16),
        vmem((16, 2, 16, FEAT), BF16),
        vmem((64, HQ), BF16),
        vmem((NX, 256, HQ), BF16),
        vmem((256, HQ), F32),
        vmem((NX - 1, 256, HQ), BF16),
        vmem((NZ - 1, 64, HQ), BF16),
        vmem((NZ - 1, 64, HQ), BF16),
        vmem((256, HID), BF16),
        vmem((256, HID), BF16),
        vmem((256, HID), BF16),
        vmem((256, HID), BF16),
        vmem((4, 64, 2 * FEAT), BF16),
        vmem((2, NY, 2, 16, FEAT), BF16),
        dma((5,)),
        dma((NY, 2)), dma((NY,)),
        dma((NY, 2)), dma((NY,)),
        dma((NZ, NX)), dma((NZ, NX)),
        dma((NZ,)), dma((NZ,)),
        dma((NX,)), dma((NX,)),
        dma((NZ,)), dma((NZ,)),
        dma((NZ, NX)), dma((NZ, NX)),
        dma((NZ,)), dma((NZ,)),
        dma((NZ, NX)), dma((NZ, NX)),
        dma((2, NY, 2)), dma((2, NY)),
        dma((NY,)), dma((NY,)),
        dma((NY,)), dma((NY,)),
        dma((6,)), dma((6,)),
    ]
    shapes = ((2, 16, FEAT), (HID, FEAT), (HID, FEAT))
    args = (tokens.reshape(2, 16, FEAT), grad_out.reshape(2, 16, FEAT), pre_act, w_in, w_out)
    results = pl.pallas_call(
        kernel,
        out_shape=tuple(pltpu.VMEM(shape, BF16) for shape in shapes),
        in_specs=[pl.BlockSpec(memory_space=pltpu.HBM)] * 5,
        out_specs=(pl.BlockSpec(memory_space=pltpu.VMEM),) * 3,
        scratch_shapes=scratch,
        compiler_params=pltpu.CompilerParams(
            collective_id=0, has_side_effects=True, vmem_limit_bytes=40 * 2**20
        ),
    )(*[pltpu.with_memory_space_constraint(arg, pltpu.HBM) for arg in args])
    grad_tokens, grad_w_in, grad_w_out = pl.pallas_call(
        store_kernel,
        out_shape=tuple(pltpu.HBM(shape, BF16) for shape in shapes),
        in_specs=[pl.BlockSpec(memory_space=pltpu.VMEM)] * 3,
        out_specs=(pl.BlockSpec(memory_space=pltpu.HBM),) * 3,
        scratch_shapes=[dma((3,))],
        compiler_params=pltpu.CompilerParams(vmem_limit_bytes=8 * 2**20),
    )(*[pltpu.with_memory_space_constraint(arg, pltpu.VMEM) for arg in results])
    return grad_tokens.reshape(32, FEAT), grad_w_in, grad_w_out


def solution(mesh):
    in_specs = (P("row", "col"), P("row", "col"), P("col", "row"), P("row", "col"), P("row", "col"))
    out_specs = (P("row", "col"), P("row", "col"), P("row", "col"))
    return jax.shard_map(per_device, mesh=mesh, in_specs=in_specs, out_specs=out_specs, check_vma=False)
```

time: 75.3 us -> 63 us (0.84)
  local copies, waits for them, and re-layouts: 7.44 us -> 0 us
  Pallas kernels: 66.8 us -> 62.1 us
    unnamed x13 -> x0, local copies, waits for them, and re-layouts: 7.44 us -> none
    pallas_call x1 -> x2, Pallas kernels: 66.8 us -> 62.1 us  [the longest x1 60.7 us: per_device(): pl.pallas_call(kernel, out_shape=tuple((pltpu.VMEM(shape, BF16) for shape...]
where the time goes in v2:
time: 63 us; the launch traced here: 62.7 us
  Pallas kernels  62.1 us (99%)
  between operations  0.64 us (1%)
    pallas_call x1, Pallas kernels, per_device(): pl.pallas_call(kernel, out_shape=tuple((pltpu.VMEM(shape, BF16) for shape...  60.7 us
    pallas_call x1, Pallas kernels, per_device(): pl.pallas_call(store_kernel, out_shape=tuple((pltpu.HBM(shape, BF16) for...  1.44 us

profile of v2, /device:TPU:1, one launch (start us, length us, event | category | flops | bytes accessed | tf_op | source)
XLA Modules:
  0.0 62.7 jit_solution(15792504151585543635)
XLA Ops:
  0.6 60.7 %shard_map.76 = (bf16[2,16,384]{2,1,0:T(8,128)(2,1)S(1)}, bf16[1536,384]{1,0:T(8,128)(2,1)S(1)}, bf16[1536,384]{1,0:T(8,128)(2,1)S(1)}) custom-call(bf16[2,16,384]{2,1,0:T(8,128)(2,1)} %bitcast.3, bf16[2,16,384]{2,1,0:T(8,128)(2,1)} %bitcast.4, bf16[16,1536]{1,0:T(8,128)(2,1)} %pre_hbm.1, bf16[1536,384]{1,0:T(8,128)(2,1)} %win_hbm.1, bf16[1536,384]{1,0:T(8,128)(2,1)} %wout_hbm.1), custom_call_target="tpu_custom_call" | custom-call | tf_op jit(solution)/shard_map/pallas_call | solution.py:308
  61.3 1.4 %shard_map.77 = (bf16[2,16,384]{2,1,0:T(8,128)(2,1)}, bf16[1536,384]{1,0:T(8,128)(2,1)}, bf16[1536,384]{1,0:T(8,128)(2,1)}) custom-call(bf16[2,16,384]{2,1,0:T(8,128)(2,1)S(1)} %get-tuple-element.9.refs_0_, bf16[1536,384]{1,0:T(8,128)(2,1)S(1)} %get-tuple-element.10.refs_1_, bf16[1536,384]{1,0:T(8,128)(2,1)S(1)} %get-tuple-element.11.refs_2_), custom_call_target="tpu_custom_call" | custom-call | tf_op jit(solution)/shard_map/pallas_call | solution.py:318

commit v3 on v2

v3 whole, which is shorter than its diff:
```python
import jax
import jax.numpy as jnp
from jax import lax
from jax.experimental import pallas as pl
from jax.experimental.pallas import tpu as pltpu
from jax.sharding import PartitionSpec as P

tanh_scale = 0.7978845608028654
cubic_term = 0.044715

MESH = pl.DeviceIdType.MESH
F32 = jnp.float32
BF16 = jnp.bfloat16
NX, NZ, NY = 4, 4, 8
FEAT = 384
HID = 1536
HQ = HID // NX
FAR_FIRST = (4, 3, 5, 2, 6, 1, 7)
X_ORDER = (2, 1, 3)
Z_ORDER = (2, 1, 3)
A_ORDER = (1, 7, 2, 6, 4, 3, 5)
STEPS = (
    ((0, 0), (0, 1)), ((7, 0), (1, 0)), ((6, 0), (2, 0)), ((5, 0), (3, 0)),
    ((7, 1), (1, 1)), ((6, 1), (2, 1)), ((4, 0), (4, 1)), ((5, 1), (3, 1)),
)
SLOTS = {block: 2 * step + index for step, blocks in enumerate(STEPS) for index, block in enumerate(blocks)}
RELAYS = ((7, 1), (6, 2), (5, 3), (4,))
STARTS = (0, 5, 9, 13, 17)


def block_slot(d, far):
    return SLOTS[d, far]


def block_rows(d, far):
    return pl.ds(16 * block_slot(d, far), 16)


def step_rows(step):
    return pl.ds(32 * step, 32)


def gelu_hidden(u):
    q = jnp.tanh(tanh_scale * (u + cubic_term * u * u * u))
    return 0.5 * u * (1.0 + q)


def gelu_slope(u):
    q = jnp.tanh(tanh_scale * (u + cubic_term * u * u * u))
    return 0.5 * (1.0 + q) + 0.5 * u * (1.0 - q * q) * tanh_scale * (1.0 + 3.0 * cubic_term * u * u)


def kernel(
    tok_hbm, go_hbm, pre_hbm, win_hbm, wout_hbm,
    gt_out, gwi_out, gwo_out,
    tok_own, go_own, pre_own, wo2, wi2, go, go_sib, tok, pre, pre_z, part, part_f, rx, sb, rz,
    gp, gp_sib, hid, hid_sib, fb, gy,
    local, a_s, a_r, az_s, az_r, x_s, x_r, z_s, z_r, p_s, p_r, hx_s, hx_r,
    pz_s, pz_r, ex_s, ex_r, gy_s, gy_r, t_s, t_r, c_s, c_r,
):
    r, c = lax.axis_index("row"), lax.axis_index("col")
    y, zl = r // 2, r % 2
    x, zh, k = c // 8, (c // 2) % NZ, c % 2

    def dev(dy=0, dzl=0, dx=0, dz=0, core=None):
        yy, ll = (y + dy) % NY, (zl + dzl) % 2
        xx, hh = (x + dx) % NX, (zh + dz) % NZ
        kk = k if core is None else core
        return (yy * 2 + ll, (xx * NZ + hh) * 2 + kk)

    def slot(yy, ll):
        d, far = (yy + NY - y) % NY, (ll + zl) % 2
        near = jnp.minimum(d, NY - d)
        ring = 2 * near + jnp.where(d < 4, 1, 0) + far * jnp.where(near == 3, 8, 6)
        return jnp.where(near == 0, far, jnp.where(near == 4, 12 + far, ring))

    def rows(start, size):
        return pl.ds(pl.multiple_of(start, 16), size)

    def cols(index, size):
        return pl.ds(pl.multiple_of(index * size, 128), size)

    sends = []

    def send(src, dst, ssem, rsem, to):
        cp = pltpu.make_async_remote_copy(
            src_ref=src, dst_ref=dst, send_sem=ssem, recv_sem=rsem, device_id=to, device_id_type=MESH
        )
        cp.start()
        sends.append((src, ssem))

    def arrived(ref, sem):
        pltpu.make_async_copy(ref, ref, sem).wait()

    def hid_rows(xx, hh):
        return rows(16 * slot(2 * xx + hh // 2, hh % 2), 16)

    sib = dev(core=1 - k)

    peers = [dev(dy=d, core=kk) for d in range(1, NY) for kk in range(2)]
    peers += [dev(dzl=1, core=kk) for kk in range(2)] + [sib]
    peers += [dev(dx=d) for d in range(1, NX)] + [dev(dz=d) for d in range(1, NZ)]
    barrier = pltpu.get_barrier_semaphore()
    for to in peers:
        pl.semaphore_signal(barrier, inc=1, device_id=to, device_id_type=MESH)

    loads = [
        pltpu.make_async_copy(pre_hbm, pre_own, local.at[0]),
        pltpu.make_async_copy(go_hbm, go_own, local.at[1]),
        pltpu.make_async_copy(tok_hbm, tok_own, local.at[2]),
        pltpu.make_async_copy(wout_hbm, wo2.at[:, cols(k, FEAT)], local.at[3]),
        pltpu.make_async_copy(win_hbm, wi2.at[:, cols(k, FEAT)], local.at[4]),
    ]
    for cp in loads:
        cp.start()
    loads[0].wait()
    loads[1].wait()
    my_rows = hid_rows(x, zh)
    hid[my_rows, :] = gelu_hidden(pre_own[...].astype(F32)).astype(BF16)
    pre_z[zh] = pre_own[...]
    go[block_rows(0, 0), cols(k, FEAT)] = go_own[k]
    pl.semaphore_wait(barrier, len(peers))

    send(wout_hbm, wo2.at[:, cols(k, FEAT)], c_s.at[1], c_r.at[1], sib)
    send(go_own.at[1 - k], go.at[block_rows(0, 0), cols(k, FEAT)], c_s.at[0], c_r.at[0], sib)
    for kk in range(2):
        send(go_own.at[kk], go.at[block_rows(0, 1), cols(k, FEAT)], az_s.at[0, kk], az_r.at[0], dev(dzl=1, core=kk))
    for d in A_ORDER:
        for kk in range(2):
            send(
                go_own.at[kk], go.at[block_rows(d, 0), cols(k, FEAT)], a_s.at[d, kk], a_r.at[d],
                dev(dy=NY - d, core=kk),
            )
    loads[2].wait()
    tok[block_slot(0, 0)] = tok_own[...]
    send(tok_own, tok.at[block_slot(0, 1)], t_s.at[1, 0], t_r.at[1, 0], dev(dzl=1))
    for d in Z_ORDER:
        send(pre_own, pre_z.at[zh], p_s.at[d], p_r.at[d], dev(dz=d))
    for d in X_ORDER:
        send(hid.at[my_rows], hid.at[my_rows], hx_s.at[0, d], hx_r.at[0, d], dev(dx=d))

    toward = 1 - 2 * (zh % 2)
    neighbours = (toward, NZ - toward)

    def partial_sums(step):
        for d, far in STEPS[step]:
            if far:
                arrived(go.at[block_rows(d, 1), :], az_r.at[d])
            elif not d:
                arrived(go.at[block_rows(0, 0), cols(1 - k, FEAT)], c_r.at[0])
        if step == 0:
            loads[3].wait()
            arrived(wo2.at[:, cols(1 - k, FEAT)], c_r.at[1])
        t = step_rows(step)
        for dx in X_ORDER + (0,):
            xx = (x + dx) % NX
            product = lax.dot_general(
                go[t, :], wo2[rows(HQ * xx, HQ), :], (((1,), (1,)), ((), ())), preferred_element_type=F32
            )
            if dx:
                part[xx, t, :] = product.astype(BF16)
                send(part.at[xx, t], rx.at[dx - 1, t], x_s.at[step, dx], x_r.at[step, dx], dev(dx=dx))
            else:
                part_f[t, :] = product
        for d in RELAYS[step] if step < len(RELAYS) else ():
            arrived(go.at[block_rows(d, 0), :], a_r.at[d])
            send(go.at[block_rows(d, 0), :], go.at[block_rows(d, 1), :], az_s.at[d, 0], az_r.at[d], dev(dzl=1))

    def exchange(step, turn, total):
        t = step_rows(step)
        part_f[t, :] = total
        sb[turn, t, :] = total.astype(BF16)
        to = dev(dz=neighbours[(step + turn) % 2])
        send(sb.at[turn, t], rz.at[turn, t], z_s.at[step, turn], z_r.at[step, turn], to)

    def sum_over_x(step):
        t = step_rows(step)
        for dx in X_ORDER:
            arrived(rx.at[dx - 1, t], x_r.at[step, dx])
        exchange(
            step, 0, part_f[t, :] + rx[0, t, :].astype(F32) + rx[1, t, :].astype(F32) + rx[2, t, :].astype(F32)
        )

    def sum_over_pair(step):
        t = step_rows(step)
        arrived(rz.at[0, t], z_r.at[step, 0])
        exchange(step, 1, part_f[t, :] + rz[0, t, :].astype(F32))

    def times_slope(step):
        t = step_rows(step)
        slopes = []
        for d, far in STEPS[step]:
            yy, ll = (y + d) % NY, (zl + far) % 2
            slopes.append(gelu_slope(pre[yy // 2, (yy % 2) * 2 + ll].astype(F32)))
        slope = jnp.concatenate(slopes, axis=0)
        arrived(rz.at[1, t], z_r.at[step, 1])
        total = part_f[t, :] + rz[1, t, :].astype(F32)
        gp[t, cols(x, HQ)] = (total * slope).astype(BF16)
        block = gp.at[t, cols(x, HQ)]
        for dx in X_ORDER:
            send(block, block, ex_s.at[step, dx], ex_r.at[step, dx], dev(dx=dx))

    def grad_tokens_part(step):
        t = step_rows(step)
        for dx in X_ORDER:
            arrived(gp.at[t, cols((x + NX - dx) % NX, HQ)], ex_r.at[step, dx])
        fb[step] = jnp.dot(gp[t, :], wi2[...], preferred_element_type=F32).astype(BF16)
        for index, (d, far) in enumerate(STEPS[step]):
            at = pl.ds(16 * index, 16)
            for flip in range(2):
                kk = k if flip == 0 else 1 - k
                src = fb.at[step, at, cols(kk, FEAT)]
                if d or far or flip:
                    send(src, gy.at[far, d, k], gy_s.at[far, d, flip], gy_r.at[far, d], dev(dy=d, dzl=far, core=kk))
                else:
                    gy[0, 0, k] = fb[step, at, cols(kk, FEAT)]

    def hidden_on(dz):
        block = hid.at[hid_rows(x, (zh + NZ - dz) % NZ)]
        for dx in X_ORDER:
            send(block, block, hx_s.at[dz, dx], hx_r.at[dz, dx], dev(dx=dx))

    def others():
        send(go.at[:, cols(1 - k, FEAT)], go_sib, c_s.at[2], c_r.at[2], sib)
        send(win_hbm, wi2.at[:, cols(k, FEAT)], c_s.at[3], c_r.at[3], sib)
        for dz in (1, 3, 2):
            arrived(pre_z.at[(zh + NZ - dz) % NZ], p_r.at[dz])
        pre[x] = pre_z[:, :, cols(x, HQ)]
        for d in X_ORDER:
            send(pre_z.at[:, :, cols((x + d) % NX, HQ)], pre.at[x], pz_s.at[d], pz_r.at[d], dev(dx=d))
        for dz in (1, 3, 2):
            there = (zh + NZ - dz) % NZ
            hid[hid_rows(x, there), :] = gelu_hidden(pre_z[there].astype(F32)).astype(BF16)
        hidden_on(1)
        arrived(tok.at[block_slot(0, 1)], t_r.at[1, 0])
        for far in range(2):
            for d in FAR_FIRST:
                send(
                    tok.at[block_slot(0, far)], tok.at[block_slot(d, far)], t_s.at[far, d], t_r.at[far, d],
                    dev(dy=NY - d),
                )

    stages = (partial_sums, sum_over_x, sum_over_pair, times_slope, grad_tokens_part)
    for tick in range(STARTS[-1] + len(STEPS)):
        if tick == STARTS[3]:
            for d in X_ORDER:
                arrived(pre.at[(x + NX - d) % NX], pz_r.at[d])
        if tick == STARTS[4]:
            loads[4].wait()
            arrived(wi2.at[:, cols(1 - k, FEAT)], c_r.at[3])
        for index in range(len(stages)):
            if 0 <= tick - STARTS[index] < len(STEPS):
                stages[index](tick - STARTS[index])
        if tick == 7:
            others()
        if tick == STARTS[3] + 7:
            hidden_on(3)
            hidden_on(2)
    send(gp, gp_sib, c_s.at[5], c_r.at[5], sib)

    over_tokens = (((0,), (0,)), ((), ()))
    for dz in range(NZ):
        for dx in X_ORDER:
            arrived(hid.at[hid_rows((x + NX - dx) % NX, (zh + NZ - dz) % NZ)], hx_r.at[dz, dx])
    send(hid, hid_sib, c_s.at[4], c_r.at[4], sib)
    for far in range(2):
        for d in FAR_FIRST:
            arrived(tok.at[block_slot(d, far)], t_r.at[far, d])
    arrived(gp_sib, c_r.at[5])
    tok_mine = tok[:, k].reshape(256, FEAT)
    tok_other = tok[:, 1 - k].reshape(256, FEAT)
    for h in range(0, HID, 256):
        a = lax.dot_general(gp[:, h : h + 256], tok_mine, over_tokens, preferred_element_type=F32)
        b = lax.dot_general(gp_sib[:, h : h + 256], tok_other, over_tokens, preferred_element_type=F32)
        gwi_out[h : h + 256, :] = (a + b).astype(BF16)
    arrived(go_sib, c_r.at[2])
    arrived(hid_sib, c_r.at[4])
    for h in range(0, HID, 256):
        a = lax.dot_general(hid[:, h : h + 256], go[:, cols(k, FEAT)], over_tokens, preferred_element_type=F32)
        b = lax.dot_general(hid_sib[:, h : h + 256], go_sib[...], over_tokens, preferred_element_type=F32)
        gwo_out[h : h + 256, :] = (a + b).astype(BF16)
    for src, ssem in sends:
        arrived(src, ssem)
    arrived(gy.at[0, 0, 1 - k], gy_r.at[0, 0])
    total = gy[0, 0].astype(F32)
    for far in range(2):
        for d in FAR_FIRST + ((0,) if far else ()):
            arrived(gy.at[far, d], gy_r.at[far, d])
            total += gy[far, d].astype(F32)
    gt_out[...] = total.astype(BF16)


def store_kernel(*refs):
    sem = refs[-1]
    copies = [pltpu.make_async_copy(refs[i], refs[3 + i], sem.at[i]) for i in range(3)]
    for cp in copies:
        cp.start()
    for cp in copies:
        cp.wait()


def per_device(tokens, grad_out, pre_act, w_in, w_out):
    vmem = pltpu.VMEM
    dma = pltpu.SemaphoreType.DMA
    any_space = pl.BlockSpec(memory_space=pl.ANY)
    scratch = [
        vmem((2, 16, FEAT), BF16),
        vmem((2, 16, FEAT), BF16),
        vmem((16, HID), BF16),
        vmem((HID, 2 * FEAT), BF16),
        vmem((HID, 2 * FEAT), BF16),
        vmem((256, 2 * FEAT), BF16),
        vmem((256, FEAT), BF16),
        vmem((16, 2, 16, FEAT), BF16),
        vmem((NX, NZ, 16, HQ), BF16),
        vmem((NZ, 16, HID), BF16),
        vmem((NX, 256, HQ), BF16),
        vmem((256, HQ), F32),
        vmem((NX - 1, 256, HQ), BF16),
        vmem((2, 256, HQ), BF16),
        vmem((2, 256, HQ), BF16),
        vmem((256, HID), BF16),
        vmem((256, HID), BF16),
        vmem((256, HID), BF16),
        vmem((256, HID), BF16),
        vmem((8, 32, 2 * FEAT), BF16),
        vmem((2, NY, 2, 16, FEAT), BF16),
        dma((5,)),
        dma((NY, 2)), dma((NY,)),
        dma((NY, 2)), dma((NY,)),
        dma((8, NX)), dma((8, NX)),
        dma((8, 2)), dma((8, 2)),
        dma((NX,)), dma((NX,)),
        dma((NZ, NX)), dma((NZ, NX)),
        dma((NX,)), dma((NX,)),
        dma((8, NX)), dma((8, NX)),
        dma((2, NY, 2)), dma((2, NY)),
        dma((2, NY)), dma((2, NY)),
        dma((6,)), dma((6,)),
    ]
    shapes = ((2, 16, FEAT), (HID, FEAT), (HID, FEAT))
    args = (tokens.reshape(2, 16, FEAT), grad_out.reshape(2, 16, FEAT), pre_act, w_in, w_out)
    results = pl.pallas_call(
        kernel,
        out_shape=tuple(pltpu.VMEM(shape, BF16) for shape in shapes),
        in_specs=[pl.BlockSpec(memory_space=pltpu.HBM)] * 5,
        out_specs=(pl.BlockSpec(memory_space=pltpu.VMEM),) * 3,
        scratch_shapes=scratch,
        compiler_params=pltpu.CompilerParams(
            collective_id=0, has_side_effects=True, vmem_limit_bytes=40 * 2**20
        ),
    )(*[pltpu.with_memory_space_constraint(arg, pltpu.HBM) for arg in args])
    grad_tokens, grad_w_in, grad_w_out = pl.pallas_call(
        store_kernel,
        out_shape=tuple(pltpu.HBM(shape, BF16) for shape in shapes),
        in_specs=[pl.BlockSpec(memory_space=pltpu.VMEM)] * 3,
        out_specs=(pl.BlockSpec(memory_space=pltpu.HBM),) * 3,
        scratch_shapes=[dma((3,))],
        compiler_params=pltpu.CompilerParams(vmem_limit_bytes=8 * 2**20),
    )(*[pltpu.with_memory_space_constraint(arg, pltpu.VMEM) for arg in results])
    return grad_tokens.reshape(32, FEAT), grad_w_in, grad_w_out


def solution(mesh):
    in_specs = (P("row", "col"), P("row", "col"), P("col", "row"), P("row", "col"), P("row", "col"))
    out_specs = (P("row", "col"), P("row", "col"), P("row", "col"))
    return jax.shard_map(per_device, mesh=mesh, in_specs=in_specs, out_specs=out_specs, check_vma=False)
```

time: 63 us -> 60 us (0.952)
  Pallas kernels: 62.1 us -> 59.2 us
    pallas_call x1, Pallas kernels: 60.7 us -> 57.8 us  [per_device(): pl.pallas_call(kernel, out_shape=tuple((pltpu.VMEM(shape, BF16) for shape...]
where the time goes in v3:
time: 60 us; the launch traced here: 59.9 us
  Pallas kernels  59.2 us (99%)
  between operations  0.64 us (1%)
    pallas_call x1, Pallas kernels, per_device(): pl.pallas_call(kernel, out_shape=tuple((pltpu.VMEM(shape, BF16) for shape...  57.8 us
    pallas_call x1, Pallas kernels, per_device(): pl.pallas_call(store_kernel, out_shape=tuple((pltpu.HBM(shape, BF16) for...  1.44 us

profile of v3, /device:TPU:1, one launch (start us, length us, event | category | flops | bytes accessed | tf_op | source)
XLA Modules:
  0.0 59.9 jit_solution(16728123843281788918)
XLA Ops:
  0.6 57.8 %shard_map.76 = (bf16[2,16,384]{2,1,0:T(8,128)(2,1)S(1)}, bf16[1536,384]{1,0:T(8,128)(2,1)S(1)}, bf16[1536,384]{1,0:T(8,128)(2,1)S(1)}) custom-call(bf16[2,16,384]{2,1,0:T(8,128)(2,1)} %bitcast.3, bf16[2,16,384]{2,1,0:T(8,128)(2,1)} %bitcast.4, bf16[16,1536]{1,0:T(8,128)(2,1)} %pre_hbm.1, bf16[1536,384]{1,0:T(8,128)(2,1)} %win_hbm.1, bf16[1536,384]{1,0:T(8,128)(2,1)} %wout_hbm.1), custom_call_target="tpu_custom_call" | custom-call | tf_op jit(solution)/shard_map/pallas_call | solution.py:343
  58.4 1.4 %shard_map.77 = (bf16[2,16,384]{2,1,0:T(8,128)(2,1)}, bf16[1536,384]{1,0:T(8,128)(2,1)}, bf16[1536,384]{1,0:T(8,128)(2,1)}) custom-call(bf16[2,16,384]{2,1,0:T(8,128)(2,1)S(1)} %get-tuple-element.9.refs_0_, bf16[1536,384]{1,0:T(8,128)(2,1)S(1)} %get-tuple-element.10.refs_1_, bf16[1536,384]{1,0:T(8,128)(2,1)S(1)} %get-tuple-element.11.refs_2_), custom_call_target="tpu_custom_call" | custom-call | tf_op jit(solution)/shard_map/pallas_call | solution.py:353

commit v4 on v3

--- a/solution.py
+++ b/solution.py
@@ -137,6 +137,8 @@
     for d in Z_ORDER:
         send(pre_own, pre_z.at[zh], p_s.at[d], p_r.at[d], dev(dz=d))
     for d in X_ORDER:
+        send(pre_own.at[:, cols((x + d) % NX, HQ)], pre.at[x, zh], pz_s.at[0, d], pz_r.at[0, d], dev(dx=d))
+    for d in X_ORDER:
         send(hid.at[my_rows], hid.at[my_rows], hx_s.at[0, d], hx_r.at[0, d], dev(dx=d))
 
     toward = 1 - 2 * (zh % 2)
@@ -226,8 +228,11 @@
         for dz in (1, 3, 2):
             arrived(pre_z.at[(zh + NZ - dz) % NZ], p_r.at[dz])
         pre[x] = pre_z[:, :, cols(x, HQ)]
-        for d in X_ORDER:
-            send(pre_z.at[:, :, cols((x + d) % NX, HQ)], pre.at[x], pz_s.at[d], pz_r.at[d], dev(dx=d))
+        for dz in (1, 3, 2):
+            there = (zh + NZ - dz) % NZ
+            for d in X_ORDER:
+                src = pre_z.at[there, :, cols((x + d) % NX, HQ)]
+                send(src, pre.at[x, there], pz_s.at[dz, d], pz_r.at[dz, d], dev(dx=d))
         for dz in (1, 3, 2):
             there = (zh + NZ - dz) % NZ
             hid[hid_rows(x, there), :] = gelu_hidden(pre_z[there].astype(F32)).astype(BF16)
@@ -243,8 +248,9 @@
     stages = (partial_sums, sum_over_x, sum_over_pair, times_slope, grad_tokens_part)
     for tick in range(STARTS[-1] + len(STEPS)):
         if tick == STARTS[3]:
-            for d in X_ORDER:
-                arrived(pre.at[(x + NX - d) % NX], pz_r.at[d])
+            for dz in range(NZ):
+                for d in X_ORDER:
+                    arrived(pre.at[(x + NX - d) % NX, (zh + NZ - dz) % NZ], pz_r.at[dz, d])
         if tick == STARTS[4]:
             loads[4].wait()
             arrived(wi2.at[:, cols(1 - k, FEAT)], c_r.at[3])
@@ -332,7 +338,7 @@
         dma((8, 2)), dma((8, 2)),
         dma((NX,)), dma((NX,)),
         dma((NZ, NX)), dma((NZ, NX)),
-        dma((NX,)), dma((NX,)),
+        dma((NZ, NX)), dma((NZ, NX)),
         dma((8, NX)), dma((8, NX)),
         dma((2, NY, 2)), dma((2, NY)),
         dma((2, NY)), dma((2, NY)),

time: 60 us -> 60.2 us (level)
  no operation moved by 1% of the time
where the time goes in v4:
time: 60.2 us; the launch traced here: 60.1 us
  Pallas kernels  59.4 us (99%)
  between operations  0.64 us (1%)
    pallas_call x1, Pallas kernels, per_device(): pl.pallas_call(kernel, out_shape=tuple((pltpu.VMEM(shape, BF16) for shape...  58 us
    pallas_call x1, Pallas kernels, per_device(): pl.pallas_call(store_kernel, out_shape=tuple((pltpu.HBM(shape, BF16) for...  1.44 us

profile of v4, /device:TPU:1, one launch (start us, length us, event | category | flops | bytes accessed | tf_op | source)
XLA Modules:
  0.0 60.1 jit_solution(1721266911448753370)
XLA Ops:
  0.6 58.0 %shard_map.76 = (bf16[2,16,384]{2,1,0:T(8,128)(2,1)S(1)}, bf16[1536,384]{1,0:T(8,128)(2,1)S(1)}, bf16[1536,384]{1,0:T(8,128)(2,1)S(1)}) custom-call(bf16[2,16,384]{2,1,0:T(8,128)(2,1)} %bitcast.3, bf16[2,16,384]{2,1,0:T(8,128)(2,1)} %bitcast.4, bf16[16,1536]{1,0:T(8,128)(2,1)} %pre_hbm.1, bf16[1536,384]{1,0:T(8,128)(2,1)} %win_hbm.1, bf16[1536,384]{1,0:T(8,128)(2,1)} %wout_hbm.1), custom_call_target="tpu_custom_call" | custom-call | tf_op jit(solution)/shard_map/pallas_call | solution.py:349
  58.6 1.4 %shard_map.77 = (bf16[2,16,384]{2,1,0:T(8,128)(2,1)}, bf16[1536,384]{1,0:T(8,128)(2,1)}, bf16[1536,384]{1,0:T(8,128)(2,1)}) custom-call(bf16[2,16,384]{2,1,0:T(8,128)(2,1)S(1)} %get-tuple-element.9.refs_0_, bf16[1536,384]{1,0:T(8,128)(2,1)S(1)} %get-tuple-element.10.refs_1_, bf16[1536,384]{1,0:T(8,128)(2,1)S(1)} %get-tuple-element.11.refs_2_), custom_call_target="tpu_custom_call" | custom-call | tf_op jit(solution)/shard_map/pallas_call | solution.py:359
